TPU v7x, 512 devices: a whole 4x4x16 slice. The times are simulated.
512 devices in a mesh: outer: 8 (over y, core), dp: 16 (over z), tensor: 4 (over x).
Axes of the slice: x: 4, y: 4, z: 16, core: 2. Of those that a mesh axis runs over, the one named last changes fastest.
Arguments:
- acts: bfloat16 [32768, 4096], P(('outer', 'dp'), 'tensor'), may hold values from -6 to 6
- out_grads: bfloat16 [32768, 4096], P(('outer', 'dp')), may hold values from -2.8125 to 2.8125
- error: float32 [8, 4096, 4096], P('outer', 'dp', 'tensor'), may hold values from -6 to 6
- q_warm: float32 [4096, 64], P('tensor'), may hold values from -0.09375 to 0.09375
Outputs:
- error_next: float32 [8, 4096, 4096], P('outer', 'dp', 'tensor')
- q_next: float32 [4096, 64], P('tensor')
All inputs are finite; a program needn't handle non-finite values.
Results may differ from a plain program's by a relative error of at most 0.0003.
Values may be sent and summed in bfloat16 or wider, within the bound.
A program may use at most 64 MiB of HBM per device.

v0:
```python
import jax
import jax.numpy as jnp
from jax import lax
from jax.sharding import PartitionSpec as P


def local(acts, out_grads, error, q_warm):
    high = lax.Precision.HIGHEST
    dy_rows = lax.all_to_all(out_grads, "dp", split_axis=1, concat_axis=0, tiled=True)
    contract = (((0,), (0,)), ((), ()))
    grad = lax.dot_general(
        dy_rows,
        lax.all_gather(acts, "dp", axis=0, tiled=True),
        contract,
        preferred_element_type=jnp.float32,
    )
    merged = grad + error[0]
    pods = lax.axis_size("outer")
    local_p = jnp.dot(merged, q_warm, precision=high)
    p_cols = lax.psum(local_p, "tensor")
    p_sum = lax.psum(p_cols, "outer")
    p_mean = p_sum / pods
    gram = lax.psum(jnp.dot(p_mean.T, p_mean, precision=high), "dp")
    chol = jnp.linalg.cholesky(gram)
    p_hat = jax.scipy.linalg.solve_triangular(chol, p_mean.T, lower=True).T
    local_q = lax.dot_general(
        merged, p_hat, contract, precision=high, preferred_element_type=jnp.float32
    )
    q_next = lax.psum(local_q, ("outer", "dp")) / pods
    approx = jnp.dot(p_hat, q_next.T, precision=high)
    return ((merged - approx)[None], q_next)


def solution(mesh):
    in_specs = (
        P(("outer", "dp"), "tensor"),
        P(("outer", "dp"), None),
        P("outer", "dp", "tensor"),
        P("tensor", None),
    )
    out_specs = (P("outer", "dp", "tensor"), P("tensor", None))
    return jax.shard_map(local, mesh=mesh, in_specs=in_specs, out_specs=out_specs, check_vma=False)
```

profile of v0, /device:TPU:1, one launch (start us, length us, event | category | flops | bytes accessed | tf_op | source)
XLA Modules:
  0.0 750.9 jit_solution(4176050050536194591)
XLA Ops:
  7.2 0.7 all-gather.2.cloned.1.call-update
  7.9 0.0 all-reduce.4.cloned.1.call-start
  8.0 3.3 copy.10
  11.2 127.2 %all_to_all.19 = bf16[256,16,256]{0,2,1:T(8,128)(2,1)} all-to-all(bf16[256,16,256]{0,2,1:T(8,128)(2,1)S(1)} %bitcast.26), channel_id=1, replica_groups=mesh['outer'=8,'dp'=16,'tensor'=4] {'dp'}, dimensions={1} | all-to-all | bytes 4194304 | tf_op jit(solution)/shard_map/all_to_all | solution.py:9
  138.4 2.9 copy.11
  141.3 64.6 %all-gather.2.cloned.1.call-done = bf16[4096,1024]{1,0:T(8,128)(2,1)} async-done(((bf16[256,1024]{1,0:T(8,128)(2,1)}), bf16[4096,1024]{1,0:T(8,128)(2,1)}) %all-gather.2.cloned.1.call-update) | async-done | bytes 8388624 | tf_op jit(solution)/shard_map/all_gather | solution.py:13
  205.9 6.0 convolution_add_fusion
  211.9 1.7 fusion.12
  213.6 0.0 all-reduce.6.cloned.1.call-start
  213.6 52.8 %all-reduce.4.cloned.1.call-done = f32[256,64]{0,1:T(8,128)} async-done(((f32[256,64]{0,1:T(8,128)}), f32[256,64]{0,1:T(8,128)}) %all-reduce.4.cloned.1.call-update) | async-done | bytes 65552 | tf_op jit(solution)/shard_map/psum | solution.py:20
  266.4 0.0 all-reduce.8.cloned.1.call-start
  266.5 77.7 %all-reduce.6.cloned.1.call-done = f32[256,64]{0,1:T(8,128)} async-done(((f32[256,64]{0,1:T(8,128)}), f32[256,64]{0,1:T(8,128)}) %all-reduce.6.cloned.1.call-update) | async-done | bytes 65552 | tf_op jit(solution)/shard_map/psum | solution.py:21
  344.2 1.1 fusion.3
  345.3 42.6 %psum.30 = f32[64,64]{0,1:T(8,128)S(1)} all-reduce(f32[64,64]{0,1:T(8,128)S(1)} %fusion.3), channel_id=1, replica_groups=mesh['outer'=8,'dp'=16,'tensor'=4] {'dp'}, use_global_device_ids=true, to_apply=%region_2.0 | all-reduce | flops 4096 | bytes 32768 | tf_op jit(solution)/shard_map/psum | solution.py:23
  387.9 0.1 copy.13
  388.0 5.8 cholesky.16
  393.8 0.6 compare_reduce_fusion
  394.5 0.7 fusion.5
  395.1 4.9 custom-call.7
  400.0 1.1 fusion.1
  401.2 1.5 fusion.13
  402.7 338.7 %all-reduce.8.cloned.1.call-done = f32[1024,64]{0,1:T(8,128)} async-done(((f32[1024,64]{0,1:T(8,128)}), f32[1024,64]{0,1:T(8,128)}) %all-reduce.8.cloned.1.call-update) | async-done | bytes 262160 | tf_op jit(solution)/shard_map/psum | solution.py:29
  741.4 1.0 broadcast_multiply_fusion
  742.4 2.0 fusion
  (10 shorter events, 0.1 us)
Async XLA Ops:
  7.2 204.7 %copy-start = (f32[1024,64]{0,1:T(8,128)S(1)}, f32[1024,64]{0,1:T(8,128)}, u32[]{:S(2)}) copy-start(f32[1024,64]{0,1:T(8,128)} %param.7) | copy-start | bytes 786436
  7.2 198.7 %all-gather.2.cloned.1.call-start = ((), (), s32[]{:S(2)}) async-start(), calls=%async_computation.1 | async-start | bytes 8912896 | tf_op jit(solution)/shard_map/all_gather | solution.py:13
  7.9 258.5 %all-reduce.4.cloned.1.call-start = ((), (), s32[]{:S(2)}) async-start(), calls=%async_computation.2 | async-start | bytes 131072 | tf_op jit(solution)/shard_map/psum | solution.py:20
  213.6 130.6 %all-reduce.6.cloned.1.call-start = ((), (), s32[]{:S(2)}) async-start(), calls=%async_computation.3 | async-start | bytes 131072 | tf_op jit(solution)/shard_map/psum | solution.py:21
  266.4 475.0 %all-reduce.8.cloned.1.call-start = ((), (), s32[]{:S(2)}) async-start(), calls=%async_computation.4 | async-start | bytes 524288 | tf_op jit(solution)/shard_map/psum | solution.py:29
  742.4 2.0 copy-start.1
Sparse Core Ops, SparseCore 0:
  10.1 195.7 all-gather.1
  213.7 52.6 all-reduce.3
  268.8 75.2 all-reduce.5
  402.8 338.5 all-reduce.7
where the time goes:
time: 751 us
  waiting for transfers between devices  535 us (71%)
  blocking collectives  170 us (23%)
  between operations  13.9 us (2%)
  matrix products  13.4 us (2%)
  other arithmetic  13 us (2%)
    psum x1, waiting for transfers between devices, local(): q_next = lax.psum(local_q, ('outer', 'dp')) / pods  339 us
    all_to_all x1, blocking collectives, local(): lax.all_to_all(out_grads, 'dp', split_axis=1, concat_axis=0, tiled=True)  127 us
    psum x1, waiting for transfers between devices, local(): p_sum = lax.psum(p_cols, 'outer')  77.7 us
    all_gather x1, waiting for transfers between devices, local(): lax.all_gather(acts, 'dp', axis=0, tiled=True)  64.6 us
    psum x1, waiting for transfers between devices, local(): p_cols = lax.psum(local_p, 'tensor')  52.8 us
    psum x1, blocking collectives, local(): gram = lax.psum(jnp.dot(p_mean.T, p_mean, precision=high), 'dp')  42.6 us
  transfers between devices with their start and end apart: 4, of which 4 were waited for; matrix products, arithmetic and copies ran while one was open for 1% of the time, Pallas kernels for 0%

commit v1 on v0

v1 whole, which is shorter than its diff:
```python
import functools

import jax
import jax.numpy as jnp
from jax import lax
from jax.experimental import pallas as pl
from jax.experimental.pallas import tpu as pltpu
from jax.sharding import PartitionSpec as P

MESH = pl.DeviceIdType.MESH
F32 = jnp.float32
BF16 = jnp.bfloat16
HIGH = lax.Precision.HIGHEST
NN = (((1,), (0,)), ((), ()))
NT = (((1,), (1,)), ((), ()))
TN = (((0,), (0,)), ((), ()))


def dot(a, b, dims, precision=None):
    return lax.dot_general(a, b, dims, precision=precision, preferred_element_type=F32)


def split3(a):
    hi = a.astype(BF16)
    rest = a - hi.astype(F32)
    mid = rest.astype(BF16)
    low = (rest - mid.astype(F32)).astype(BF16)
    return jnp.concatenate([hi, mid, low], axis=0)


def dot3(a, b, dims):
    k = a.shape[0]
    full = dot(split3(a), b, dims)
    return (full[2 * k :] + full[k : 2 * k]) + full[:k]


class Exchange:
    def __init__(self, axis, n, stride, slots, sems):
        self.axis, self.n, self.stride, self.slots, self.sems = axis, n, stride, slots, sems

    def start(self, source):
        size = self.n * self.stride
        me = lax.axis_index(self.axis)

        def send(d, carry):
            to = lax.rem(me + d * self.stride, size)
            pltpu.make_async_remote_copy(
                src_ref=source(to),
                dst_ref=self.slots.at[d],
                send_sem=self.sems.at[0],
                recv_sem=self.sems.at[1],
                device_id={self.axis: to},
                device_id_type=MESH,
            ).start()
            return carry

        lax.fori_loop(1, self.n, send, 0)

    def _wait(self, which):
        arrived = self.slots.at[pl.ds(1, self.n - 1)]
        pltpu.make_async_copy(arrived, arrived, self.sems.at[which]).wait()

    def wait_recv(self):
        self._wait(1)

    def wait_send(self):
        self._wait(0)


class Reduce:
    def __init__(self, n_g, n_z, part, grs, zsrc, zrs, zag, gag, sems):
        self.n_g, self.n_z, self.part, self.zsrc = n_g, n_z, part, zsrc
        self.tiles, self.width = zsrc.shape[0], zsrc.shape[2]
        self.dup = n_z // self.tiles
        self.grs = Exchange("outer", n_g, 1, grs, sems.at[0])
        self.zrs = Exchange("dp", n_z, 1, zrs, sems.at[1])
        self.zag = Exchange("dp", self.tiles, self.dup, zag, sems.at[2])
        self.gag = Exchange("outer", n_g, 1, gag, sems.at[3])

    def scatter_outer(self):
        self.grs.start(lambda to: self.part.at[to])

    def scatter_dp(self):
        self.grs.wait_recv()
        me = lax.axis_index("outer")
        self.grs.slots[0] = self.part[me]
        total = self.grs.slots[me]
        for source in range(1, self.n_g):
            total = total + self.grs.slots[lax.rem(me + self.n_g - source, self.n_g)]
        for tile in range(self.tiles):
            self.zsrc[tile] = total[:, tile * self.width : (tile + 1) * self.width]
        self.zrs.start(lambda to: self.zsrc.at[to // self.dup])

    def gather_dp(self):
        self.zrs.wait_recv()
        me = lax.axis_index("dp")
        self.zrs.slots[0] = self.zsrc[me // self.dup]
        total = self.zrs.slots[me]
        for source in range(1, self.n_z):
            total = total + self.zrs.slots[lax.rem(me + self.n_z - source, self.n_z)]
        self.zag.slots[0] = total
        self.zag.start(lambda to: self.zag.slots.at[0])

    def gather_outer(self):
        self.zag.wait_recv()
        mine = lax.axis_index("dp") // self.dup
        for tile in range(self.tiles):
            block = self.zag.slots[lax.rem(mine + self.tiles - tile, self.tiles)]
            self.gag.slots[0, :, tile * self.width : (tile + 1) * self.width] = block
        self.gag.start(lambda to: self.gag.slots.at[0])

    def finish(self):
        self.gag.wait_recv()
        me = lax.axis_index("outer")
        return jnp.concatenate(
            [self.gag.slots[lax.rem(me + self.n_g - source, self.n_g)] for source in range(self.n_g)], axis=0
        )

    def drain(self):
        for exchange in (self.grs, self.zrs, self.zag, self.gag):
            exchange.wait_send()


def kernel(
    sizes,
    acts, dy, err, q,
    out, q_out,
    held, dyv, dyall, errv, qv, wex, pfull, elim, ut,
    part_p, grs_p, zsrc_p, zrs_p, zag_p, gag_p,
    part_u, grs_u, zsrc_u, zrs_u, zag_u, gag_u,
    loc, ring_send, ring_recv, dyz_sems, dyx_sems, wex_sems, px_sems, p_sems, u_sems,
):
    n_g, n_z, n_x = sizes
    z, x = lax.axis_index("dp"), lax.axis_index("tensor")
    tok, cols = acts.shape
    rows = dy.shape[1]
    rows_z, rows_x = rows // n_z, rows // n_x
    rank = q.shape[1]
    quarter, half = tok // n_x, tok // 2
    steps = n_z // 2

    loads = [
        pltpu.make_async_copy(src, dst, loc.at[i])
        for i, (src, dst) in enumerate(((acts, held.at[0]), (q, qv), (err, errv), (dy, dyv)))
    ]
    for load in loads:
        load.start()
    my_tokens = pl.ds(pl.multiple_of(x * quarter, quarter), quarter)
    own_dy = pltpu.make_async_copy(
        dy.at[my_tokens, pl.ds(pl.multiple_of(z * rows_z, rows_z), rows_z)], dyall.at[0, my_tokens, :], loc.at[4]
    )
    own_dy.start()

    barrier = pltpu.get_barrier_semaphore()
    for axis, n in (("dp", n_z), ("tensor", n_x), ("outer", n_g)):
        def greet(d, carry, axis=axis, n=n):
            to = lax.rem(lax.axis_index(axis) + d, n)
            pl.semaphore_signal(barrier, inc=1, device_id={axis: to}, device_id_type=MESH)
            return carry

        lax.fori_loop(1, n, greet, 0)
    pl.semaphore_wait(barrier, n_z + n_x + n_g - 3)

    def chunk(slot, c):
        return held.at[slot, pl.ds(c * half, half), :]

    def ring_copy(direction, s, c):
        here, there = (s, s + 1) if direction == 0 else ((n_z - s) % n_z, n_z - s - 1)
        to = lax.rem(z + (1 if direction == 0 else n_z - 1), n_z)
        return pltpu.make_async_remote_copy(
            src_ref=acts.at[pl.ds(c * half, half), :] if s == 0 else chunk(here, c),
            dst_ref=chunk(there, c),
            send_sem=ring_send.at[direction, s, c],
            recv_sem=ring_recv.at[direction, s, c],
            device_id={"dp": to},
            device_id_type=MESH,
        )

    def sends(s, c):
        return [ring_copy(direction, s, c) for direction in range(2) if s < steps - 1 or c == direction]

    for c in range(2):
        for copy in sends(0, c):
            copy.start()

    def send_dy(d, carry):
        to = lax.rem(z + d, n_z)
        pltpu.make_async_remote_copy(
            src_ref=dy.at[my_tokens, pl.ds(pl.multiple_of(to * rows_z, rows_z), rows_z)],
            dst_ref=dyall.at[d, my_tokens, :],
            send_sem=dyz_sems.at[0],
            recv_sem=dyz_sems.at[1],
            device_id={"dp": to},
            device_id_type=MESH,
        ).start()
        return carry

    lax.fori_loop(1, n_z, send_dy, 0)

    def wait_dyz(which):
        arrived = dyall.at[pl.ds(1, n_z - 1), pl.ds(0, quarter), :]
        pltpu.make_async_copy(arrived, arrived, dyz_sems.at[which]).wait()

    def send_dyx():
        wait_dyz(1)
        own_dy.wait()

        def send(d, carry):
            mine = dyall.at[:, my_tokens, :]
            pltpu.make_async_remote_copy(
                src_ref=mine,
                dst_ref=mine,
                send_sem=dyx_sems.at[0],
                recv_sem=dyx_sems.at[1],
                device_id={"tensor": lax.rem(x + d, n_x)},
                device_id_type=MESH,
            ).start()
            return carry

        lax.fori_loop(1, n_x, send, 0)

    def wait_dyx(which):
        arrived = dyall.at[:, pl.ds(0, quarter * (n_x - 1)), :]
        pltpu.make_async_copy(arrived, arrived, dyx_sems.at[which]).wait()

    p_sum = Reduce(n_g, n_z, part_p, grs_p, zsrc_p, zrs_p, zag_p, gag_p, p_sems)
    u_sum = Reduce(n_g, n_z, part_u, grs_u, zsrc_u, zrs_u, zag_u, gag_u, u_sems)
    w_exchange = Exchange("tensor", n_x, 1, wex, wex_sems)
    p_exchange = Exchange("tensor", n_x, 1, pfull, px_sems)
    row_quarter = (z * rows_z) // rows_x
    row_start = pl.multiple_of(lax.rem(z * rows_z, rows_x), 128)

    def by_group(a):
        return a.reshape(n_g, rank // n_g, a.shape[1])

    def start_w():
        for load in loads[:3]:
            load.wait()
        qt = qv[...].T
        wex[0, :, :tok] = dot3(qt, held[0], NT)
        wex[0, :, tok:] = dot(qt, errv[...], NT, HIGH)
        w_exchange.start(lambda to: wex.at[0])

    def start_p():
        w_exchange.wait_recv()
        loads[3].wait()
        total = wex[x]
        for source in range(1, n_x):
            total = total + wex[lax.rem(x + n_x - source, n_x)]
        mine = dyv[:, pl.ds(pl.multiple_of(x * rows_x, rows_x), rows_x)]
        part_p[...] = by_group(dot3(total[:, :tok], mine, NN))

        @pl.when(x == row_quarter)
        def _():
            part_p[:, :, pl.ds(row_start, rows_z)] += by_group(total[:, tok:])

        p_sum.scatter_outer()

    def gather_p():
        pfull[0] = p_sum.finish() * (1.0 / n_g)
        p_exchange.start(lambda to: pfull.at[0])

    def p_rows():
        return pfull[lax.rem(x + n_x - row_quarter, n_x), :, pl.ds(row_start, rows_z)]

    def start_u():
        p_exchange.wait_recv()
        vt = jnp.zeros((rank, tok), F32)
        gram = jnp.zeros((rank, rank), F32)
        for source in range(n_x):
            p = pfull[lax.rem(x + n_x - source, n_x)]
            vt += dot3(p, dyv[:, source * rows_x : (source + 1) * rows_x], NT)
            gram += dot(p, p, NT, HIGH)
        part_u[...] = by_group(dot3(vt, held[0], NN) + dot(p_rows(), errv[...], NN, HIGH))
        u_sum.scatter_outer()
        row = lax.broadcasted_iota(jnp.int32, (rank, rank), 0)
        col = lax.broadcasted_iota(jnp.int32, (rank, rank), 1)
        elim[:, :rank] = (row == col).astype(F32)
        elim[:, rank:] = gram

    def eliminate(first, last):
        row = lax.broadcasted_iota(jnp.int32, (rank, 2 * rank), 0)
        lane = lax.broadcasted_iota(jnp.int32, (rank, 2 * rank), 1)
        lane1 = lax.broadcasted_iota(jnp.int32, (1, 2 * rank), 1)

        def column(j, carry):
            whole = elim[...]
            pivot_row = elim[pl.ds(j, 1), :]
            pivot = jnp.sum(jnp.where(lane1 == rank + j, pivot_row, 0.0), axis=1, keepdims=True)
            scale = 1.0 / jnp.sqrt(pivot)
            pivot_row = pivot_row * scale
            factor = jnp.sum(jnp.where(lane == rank + j, whole, 0.0), axis=1, keepdims=True) * scale
            elim[...] = jnp.where(row > j, whole - factor * pivot_row, jnp.where(row == j, pivot_row, whole))
            return carry

        lax.fori_loop(first, last, column, 0)

    def finish_u():
        ut[...] = u_sum.finish()

    def correct():
        inverse = elim[:, :rank]
        qt = dot(inverse, ut[...], NN, HIGH) * (1.0 / n_g)
        pt = dot(inverse, p_rows(), NN, HIGH)
        ut[...] = qt
        pltpu.make_async_copy(ut, q_out, loc.at[0]).start()
        p_hi, q_hi = pt.astype(BF16), qt.astype(BF16)
        p_lo, q_lo = (pt - p_hi.astype(F32)).astype(BF16), (qt - q_hi.astype(F32)).astype(BF16)
        left = jnp.concatenate([p_hi, p_hi, p_lo], axis=0)
        right = jnp.concatenate([q_hi, q_lo, q_hi], axis=0)
        errv[...] -= dot(left, right, TN)

    def add(slot):
        errv[...] += dot(dyall[slot], held[slot], TN)

    def add_ring(*distances):
        for d in distances:
            for slot in sorted({d, (n_z - d) % n_z}):
                add(slot)

    last = 2 * steps - 1
    work = [
        (2, p_sum.scatter_dp),
        (3, p_sum.gather_dp),
        (4, p_sum.gather_outer),
        (5, gather_p),
        (5, send_dyx),
        (7, start_u),
        (8, u_sum.scatter_dp),
        (9, u_sum.gather_dp),
        (10, u_sum.gather_outer),
        (11, finish_u),
        (11, lambda: wait_dyx(1)),
    ]
    pieces = 5
    for i in range(pieces):
        work.append((9 + i, functools.partial(eliminate, rank * i // pieces, rank * (i + 1) // pieces)))
    work.append((12, lambda: add_ring(*range(0, steps // 2))))
    work.append((13, lambda: add_ring(*range(steps // 2, steps - 1))))
    work.append((14, correct))

    start_w()
    start_p()
    for t in range(2, last + 1):
        s, c = t // 2, t % 2
        for copy in sends(s - 1, c):
            copy.wait_recv()
        for copy in sends(s, c):
            copy.start()
        for at, do in work:
            if at == t or (t == last and at > last):
                do()
    add_ring(steps - 1)
    for c in range(2):
        for copy in sends(steps - 1, c):
            copy.wait_recv()
    add(steps)
    result = pltpu.make_async_copy(errv, out, loc.at[1])
    result.start()

    for s in range(steps):
        for c in range(2):
            for copy in sends(s, c):
                copy.wait_send()
    wait_dyz(0)
    wait_dyx(0)
    w_exchange.wait_send()
    p_exchange.wait_send()
    p_sum.drain()
    u_sum.drain()
    pltpu.make_async_copy(ut, q_out, loc.at[0]).wait()
    result.wait()


def local(sizes, acts, out_grads, error, q_warm):
    n_g, n_z, n_x = sizes
    tok, cols = acts.shape
    rows = out_grads.shape[1]
    rows_z, rows_x = rows // n_z, rows // n_x
    rank = q_warm.shape[1]
    group = rank // n_g

    def reduce_scratch(width):
        tile = max(128, width // n_z)
        return [
            pltpu.VMEM((n_g, group, width), F32),
            pltpu.VMEM((n_g, group, width), F32),
            pltpu.VMEM((width // tile, group, tile), F32),
            pltpu.VMEM((n_z, group, tile), F32),
            pltpu.VMEM((width // tile, group, tile), F32),
            pltpu.VMEM((n_g, group, width), F32),
        ]

    anywhere = pl.BlockSpec(memory_space=pl.ANY)
    dma = pltpu.SemaphoreType.DMA
    new_error, q_next = pl.pallas_call(
        functools.partial(kernel, sizes),
        out_shape=(
            jax.ShapeDtypeStruct((rows_z, cols), F32),
            jax.ShapeDtypeStruct((rank, cols), F32),
        ),
        in_specs=[anywhere] * 4,
        out_specs=(anywhere, anywhere),
        scratch_shapes=[
            pltpu.VMEM((n_z, tok, cols), BF16),
            pltpu.VMEM((tok, rows), BF16),
            pltpu.VMEM((n_z, tok, rows_z), BF16),
            pltpu.VMEM((rows_z, cols), F32),
            pltpu.VMEM((cols, rank), F32),
            pltpu.VMEM((n_x, rank, tok + rows_z), F32),
            pltpu.VMEM((n_x, rank, rows_x), F32),
            pltpu.VMEM((rank, 2 * rank), F32),
            pltpu.VMEM((rank, cols), F32),
            *reduce_scratch(rows_x),
            *reduce_scratch(cols),
            dma((5,)),
            dma((2, n_z // 2, 2)),
            dma((2, n_z // 2, 2)),
            dma((2,)),
            dma((2,)),
            dma((2,)),
            dma((2,)),
            dma((4, 2)),
            dma((4, 2)),
        ],
        compiler_params=pltpu.CompilerParams(
            collective_id=0, has_side_effects=True, vmem_limit_bytes=48 * 1024 * 1024
        ),
        cost_estimate=pl.CostEstimate(
            flops=2 * rows_z * cols * tok * n_z, bytes_accessed=2 * tok * (cols + rows) + 8 * rows_z * cols, transcendentals=0
        ),
        name="powersgd_step",
    )(acts, out_grads, error[0], q_warm)
    return new_error[None], q_next.T


def solution(mesh):
    sizes = (mesh.shape["outer"], mesh.shape["dp"], mesh.shape["tensor"])
    in_specs = (
        P(("outer", "dp"), "tensor"),
        P(("outer", "dp"), None),
        P("outer", "dp", "tensor"),
        P("tensor", None),
    )
    out_specs = (P("outer", "dp", "tensor"), P("tensor", None))
    return jax.shard_map(
        functools.partial(local, sizes), mesh=mesh, in_specs=in_specs, out_specs=out_specs, check_vma=False
    )
```

time: 751 us -> 154 us (0.21)
  waiting for transfers between devices: 535 us -> 0 us
  blocking collectives: 170 us -> 0 us
  Pallas kernels: 0 us -> 146 us
  matrix products: 13.4 us -> 0 us
  between operations: 13.9 us -> 0.66 us
  other arithmetic: 13 us -> 0 us
    psum x3 -> x0, waiting for transfers between devices: 469 us -> none  [the longest x1 339 us: local(): q_next = lax.psum(local_q, ('outer', 'dp')) / pods]
    pallas_call x0 -> x1, Pallas kernels: none -> 146 us  [local(): pl.pallas_call(functools.partial(kernel, sizes), out_shape=(jax.ShapeDtyp...]
    all_to_all x1 -> x0, blocking collectives: 127 us -> none  [local(): lax.all_to_all(out_grads, 'dp', split_axis=1, concat_axis=0, tiled=True)]
    all_gather x1 -> x0, waiting for transfers between devices: 64.6 us -> none  [local(): lax.all_gather(acts, 'dp', axis=0, tiled=True)]
    psum x1 -> x0, blocking collectives: 42.6 us -> none  [local(): gram = lax.psum(jnp.dot(p_mean.T, p_mean, precision=high), 'dp')]
    dot_general x5 -> x0, matrix products: 12.3 us -> none  [the longest x1 5.97 us: local(): lax.dot_general(dy_rows, lax.all_gather(acts, 'dp', axis=0, tiled=True),...]
    another operation x5 -> x0, other arithmetic: 12.1 us -> none  [the longest x3 6.52 us: local(): chol = jnp.linalg.cholesky(gram)]
  transfers between devices with their start and end apart: 4 -> 0, of which waited for: 4 -> 0; matrix products, arithmetic and copies ran while one was open for 1% -> 0% of each run, Pallas kernels for 0% -> 0%
where the time goes in v1:
time: 154 us; the launch traced here: 153 us
  Pallas kernels  146 us (95%)
  local copies, waits for them, and re-layouts  6.67 us (4%)
    pallas_call x1, Pallas kernels, local(): pl.pallas_call(functools.partial(kernel, sizes), out_shape=(jax.ShapeDtyp...  146 us
    unnamed x9, local copies, waits for them, and re-layouts  6.67 us

profile of v1, /device:TPU:1, one launch (start us, length us, event | category | flops | bytes accessed | tf_op | source)
XLA Modules:
  0.0 153.4 jit_solution(15556347606028264171)
XLA Ops:
  0.6 1.1 copy.6.q
  1.8 0.0 copy-start
  1.8 1.6 %copy-done = bf16[256,4096]{1,0:T(8,128)(2,1)S(1)} copy-done((bf16[256,4096]{1,0:T(8,128)(2,1)S(1)}, bf16[256,4096]{1,0:T(8,128)(2,1)}, u32[]{:S(2)}) %copy-start) | copy-done | bytes 2097176
  3.4 0.0 copy-start.1
  3.4 1.2 copy-done.1
  4.6 0.0 copy-start.2
  4.6 1.0 copy-done.2
  5.6 146.1 %powersgd_step.1 = (f32[256,1024]{1,0:T(8,128)S(1)}, f32[64,1024]{1,0:T(8,128)S(1)}) custom-call(bf16[256,1024]{1,0:T(8,128)(2,1)S(1)} %copy-done.2, bf16[256,4096]{1,0:T(8,128)(2,1)S(1)} %copy-done, f32[256,1024]{1,0:T(8,128)S(1)} %bitcast.5, f32[1024,64]{1,0:T(8,128)S(1)} %copy.6.q), custom_call_target="tpu_custom_call" | custom-call | flops 2147483648 | bytes 4718592 | tf_op jit(solution)/shard_map/powersgd_step/pallas_call | solution.py:396
  151.7 1.0 copy.9
  152.7 0.7 copy.10
Async XLA Ops:
  1.8 1.6 %copy-start = (bf16[256,4096]{1,0:T(8,128)(2,1)S(1)}, bf16[256,4096]{1,0:T(8,128)(2,1)}, u32[]{:S(2)}) copy-start(bf16[256,4096]{1,0:T(8,128)(2,1)} %dy.1) | copy-start | bytes 6291460
  3.4 1.2 copy-start.1
  4.6 1.0 copy-start.2

commit v2 on v1

v2 whole, which is shorter than its diff:
```python
import functools

import jax
import jax.numpy as jnp
from jax import lax
from jax.experimental import pallas as pl
from jax.experimental.pallas import tpu as pltpu
from jax.sharding import PartitionSpec as P

MESH = pl.DeviceIdType.MESH
VMEM = 62
CHUNKS = 4
RIGHT = 2
F32 = jnp.float32
BF16 = jnp.bfloat16
HIGH = lax.Precision.HIGHEST
NN = (((1,), (0,)), ((), ()))
NT = (((1,), (1,)), ((), ()))
TN = (((0,), (0,)), ((), ()))


def dot(a, b, dims, precision=None):
    return lax.dot_general(a, b, dims, precision=precision, preferred_element_type=F32)


def split3(a):
    hi = a.astype(BF16)
    rest = a - hi.astype(F32)
    mid = rest.astype(BF16)
    low = (rest - mid.astype(F32)).astype(BF16)
    return jnp.concatenate([hi, mid, low], axis=0)


def dot3(a, b, dims):
    k = a.shape[0]
    full = dot(split3(a), b, dims)
    return (full[2 * k :] + full[k : 2 * k]) + full[:k]


class Exchange:
    def __init__(self, axis, n, slots, sems):
        self.axis, self.n, self.slots, self.sems = axis, n, slots, sems

    def me(self):
        return lax.axis_index(self.axis)

    def get(self, source):
        return self.slots[lax.rem(self.me() + self.n - source, self.n)]

    def start(self, source):
        def send(d, carry):
            to = lax.rem(self.me() + d, self.n)
            pltpu.make_async_remote_copy(
                src_ref=source(to),
                dst_ref=self.slots.at[d],
                send_sem=self.sems.at[0],
                recv_sem=self.sems.at[1],
                device_id={self.axis: to},
                device_id_type=MESH,
            ).start()
            return carry

        lax.fori_loop(1, self.n, send, 0)

    def _wait(self, which):
        arrived = self.slots.at[pl.ds(1, self.n - 1)]
        pltpu.make_async_copy(arrived, arrived, self.sems.at[which]).wait()

    def wait_recv(self):
        self._wait(1)

    def wait_send(self):
        self._wait(0)


class Reduce:
    def __init__(self, n_g, n_z, part, grs, zsrc, zrs, zag, gag, sems):
        self.n_g, self.n_z, self.part, self.zsrc = n_g, n_z, part, zsrc
        self.height, self.width = zsrc.shape[1:]
        self.across = part.shape[2] // self.width
        self.grs = Exchange("outer", n_g, grs, sems.at[0])
        self.zrs = Exchange("dp", n_z, zrs, sems.at[1])
        self.zag = Exchange("dp", n_z, zag, sems.at[2])
        self.gag = Exchange("outer", n_g, gag, sems.at[3])

    def place(self, piece):
        down, right = piece // self.across * self.height, piece % self.across * self.width
        return slice(down, down + self.height), slice(right, right + self.width)

    def scatter_outer(self):
        self.grs.start(lambda to: self.part.at[to])

    def scatter_dp(self):
        self.grs.wait_recv()
        self.grs.slots[0] = self.part[self.grs.me()]
        total = self.grs.get(0)
        for source in range(1, self.n_g):
            total = total + self.grs.get(source)
        for piece in range(self.n_z):
            self.zsrc[piece] = total[self.place(piece)]
        self.zrs.start(lambda to: self.zsrc.at[to])

    def gather_dp(self):
        self.zrs.wait_recv()
        self.zrs.slots[0] = self.zsrc[self.zrs.me()]
        total = self.zrs.get(0)
        for source in range(1, self.n_z):
            total = total + self.zrs.get(source)
        self.zag.slots[0] = total
        self.zag.start(lambda to: self.zag.slots.at[0])

    def gather_outer(self):
        self.zag.wait_recv()
        for piece in range(self.n_z):
            self.gag.slots[(0, *self.place(piece))] = self.zag.get(piece)
        self.gag.start(lambda to: self.gag.slots.at[0])

    def finish(self):
        self.gag.wait_recv()
        return [self.gag.get(source) for source in range(self.n_g)]

    def drain(self):
        for exchange in (self.grs, self.zrs, self.zag, self.gag):
            exchange.wait_send()


def kernel(
    sizes,
    acts, dy, err, q,
    out, q_out,
    held, dyv, dyall, qv, wsrc, wex, vex, gex, pfull, prow, elim,
    part_p, grs_p, zsrc_p, zrs_p, zag_p, gag_p,
    part_u, grs_u, zsrc_u, zrs_u, zag_u, gag_u,
    loc, ring_send, ring_recv, dyz_sems, dyx_sems, wex_sems, vex_sems, gram_sems, p_sems, u_sems,
):
    n_g, n_z, n_x = sizes
    z, x = lax.axis_index("dp"), lax.axis_index("tensor")
    tok, cols = acts.shape
    rows = dy.shape[1]
    rows_z = rows // n_z
    rank = q.shape[0]
    quarter, part = tok // n_x, tok // CHUNKS
    steps = n_z // 2

    loads = [
        pltpu.make_async_copy(src, dst, loc.at[i])
        for i, (src, dst) in enumerate(((acts, held.at[0]), (q, qv), (err, out), (dy, dyv)))
    ]
    for load in loads:
        load.start()
    my_tokens = pl.ds(pl.multiple_of(x * quarter, quarter), quarter)
    own_dy = pltpu.make_async_copy(
        dy.at[my_tokens, pl.ds(pl.multiple_of(z * rows_z, rows_z), rows_z)], dyall.at[0, my_tokens, :], loc.at[4]
    )
    own_dy.start()

    barrier = pltpu.get_barrier_semaphore()
    for axis, n in (("dp", n_z), ("tensor", n_x), ("outer", n_g)):
        def greet(d, carry, axis=axis, n=n):
            to = lax.rem(lax.axis_index(axis) + d, n)
            pl.semaphore_signal(barrier, inc=1, device_id={axis: to}, device_id_type=MESH)
            return carry

        lax.fori_loop(1, n, greet, 0)
    pl.semaphore_wait(barrier, n_z + n_x + n_g - 3)

    def chunk(slot, c):
        return held.at[slot, pl.ds(c * part, part), :]

    def ring_copy(direction, s, c):
        here, there = (s, s + 1) if direction == 0 else ((n_z - s) % n_z, n_z - s - 1)
        to = lax.rem(z + (1 if direction == 0 else n_z - 1), n_z)
        return pltpu.make_async_remote_copy(
            src_ref=acts.at[pl.ds(c * part, part), :] if s == 0 else chunk(here, c),
            dst_ref=chunk(there, c),
            send_sem=ring_send.at[direction, s, c],
            recv_sem=ring_recv.at[direction, s, c],
            device_id={"dp": to},
            device_id_type=MESH,
        )

    def sends(s, c):
        return [ring_copy(direction, s, c) for direction in range(2) if s < steps - 1 or (c < RIGHT) == (direction == 0)]

    for c in range(CHUNKS):
        for copy in sends(0, c):
            copy.start()

    def send_dy(d, carry):
        to = lax.rem(z + d, n_z)
        pltpu.make_async_remote_copy(
            src_ref=dy.at[my_tokens, pl.ds(pl.multiple_of(to * rows_z, rows_z), rows_z)],
            dst_ref=dyall.at[d, my_tokens, :],
            send_sem=dyz_sems.at[0],
            recv_sem=dyz_sems.at[1],
            device_id={"dp": to},
            device_id_type=MESH,
        ).start()
        return carry

    lax.fori_loop(1, n_z, send_dy, 0)

    def wait_dyz(which):
        arrived = dyall.at[pl.ds(1, n_z - 1), pl.ds(0, quarter), :]
        pltpu.make_async_copy(arrived, arrived, dyz_sems.at[which]).wait()

    def send_dyx(piece):
        if piece == 0:
            wait_dyz(1)
            own_dy.wait()

        def send(d, carry):
            mine = dyall.at[pl.ds(piece * steps, steps), my_tokens, :]
            pltpu.make_async_remote_copy(
                src_ref=mine,
                dst_ref=mine,
                send_sem=dyx_sems.at[0, piece],
                recv_sem=dyx_sems.at[1, piece],
                device_id={"tensor": lax.rem(x + d, n_x)},
                device_id_type=MESH,
            ).start()
            return carry

        lax.fori_loop(1, n_x, send, 0)

    def wait_dyx(which):
        for piece in range(2):
            arrived = dyall.at[pl.ds(piece * steps, steps), pl.ds(0, quarter * (n_x - 1)), :]
            pltpu.make_async_copy(arrived, arrived, dyx_sems.at[which, piece]).wait()

    p_sum = Reduce(n_g, n_z, part_p, grs_p, zsrc_p, zrs_p, zag_p, gag_p, p_sems)
    u_sum = Reduce(n_g, n_z, part_u, grs_u, zsrc_u, zrs_u, zag_u, gag_u, u_sems)
    w_exchange = Exchange("tensor", n_x, wex, wex_sems)
    v_exchange = Exchange("tensor", n_x, vex, vex_sems)
    gram_exchange = Exchange("outer", n_g, gex, gram_sems)
    wide = rows // n_g
    my_rows = pl.ds(pl.multiple_of(z * rows_z, rows_z), rows_z)

    def start_w():
        for load in loads[:3]:
            load.wait()
        qt = qv[...]
        wsrc[:, :, :tok] = dot3(qt, held[0], NT).reshape(n_x, rank // n_x, tok)
        wsrc[:, :, tok:] = dot(qt, out[...], NT, HIGH).reshape(n_x, rank // n_x, rows_z)
        w_exchange.start(lambda to: wsrc.at[to])

    def start_p():
        w_exchange.wait_recv()
        loads[3].wait()
        wex[0] = wsrc[x]
        total = w_exchange.get(0)
        for source in range(1, n_x):
            total = total + w_exchange.get(source)
        pt = dot3(total[:, :tok], dyv[...], NN)
        for group in range(n_g):
            part_p[group] = pt[:, group * wide : (group + 1) * wide]
        mine = z * rows_z
        part_p[mine // wide, :, pl.ds(pl.multiple_of(lax.rem(mine, wide), 128), rows_z)] += total[:, tok:]
        p_sum.scatter_outer()

    def gather_p():
        pt = jnp.concatenate(p_sum.finish(), axis=1) * (1.0 / n_g)
        pfull[...] = pt
        vex[0, :, :tok] = dot3(pt, dyv[...], NT)
        vex[0, :, tok : tok + rows_z] = pfull[:, my_rows]
        vex[0, :, tok + rows_z :] = gag_p[0] * (1.0 / n_g)
        v_exchange.start(lambda to: vex.at[0])

    def start_u():
        v_exchange.wait_recv()
        vr = jnp.concatenate([v_exchange.get(source) for source in range(n_x)], axis=0)
        own_rows, some_rows = vr[:, tok : tok + rows_z], vr[:, tok + rows_z :]
        prow[...] = own_rows
        ut = dot3(vr[:, :tok], held[0], NN) + dot(own_rows, out[...], NN, HIGH)
        part_u[...] = ut.reshape(n_g, rank // n_g, cols)
        u_sum.scatter_outer()
        gram = dot(some_rows, some_rows, NT, HIGH)
        gex[0] = jnp.concatenate([gram, jnp.zeros_like(gram)], axis=1)
        gram_exchange.start(lambda to: gex.at[0])

    def start_gram():
        gram_exchange.wait_recv()
        gram = gram_exchange.get(0)
        for source in range(1, n_g):
            gram = gram + gram_exchange.get(source)
        row = lax.broadcasted_iota(jnp.int32, (rank, rank), 0)
        col = lax.broadcasted_iota(jnp.int32, (rank, rank), 1)
        elim[:, :rank] = (row == col).astype(F32)
        elim[:, rank:] = gram[:, :rank]

    def eliminate(first, last):
        row = lax.broadcasted_iota(jnp.int32, (rank, 2 * rank), 0)
        lane = lax.broadcasted_iota(jnp.int32, (rank, 2 * rank), 1)
        lane1 = lax.broadcasted_iota(jnp.int32, (1, 2 * rank), 1)

        def column(j, carry):
            whole = elim[...]
            pivot_row = elim[pl.ds(j, 1), :]
            pivot = jnp.sum(jnp.where(lane1 == rank + j, pivot_row, 0.0), axis=1, keepdims=True)
            scale = 1.0 / jnp.sqrt(pivot)
            pivot_row = pivot_row * scale
            factor = jnp.sum(jnp.where(lane == rank + j, whole, 0.0), axis=1, keepdims=True) * scale
            elim[...] = jnp.where(row > j, whole - factor * pivot_row, jnp.where(row == j, pivot_row, whole))
            return carry

        lax.fori_loop(first, last, column, 0)

    def finish_u():
        q_out[...] = jnp.concatenate(u_sum.finish(), axis=0)

    def correct():
        inverse = elim[:, :rank]
        qt = dot(inverse, q_out[...], NN, HIGH) * (1.0 / n_g)
        pt = dot(inverse, prow[...], NN, HIGH)
        q_out[...] = qt
        p_hi, q_hi = pt.astype(BF16), qt.astype(BF16)
        p_lo, q_lo = (pt - p_hi.astype(F32)).astype(BF16), (qt - q_hi.astype(F32)).astype(BF16)
        left = jnp.concatenate([p_hi, p_hi, p_lo], axis=0)
        right = jnp.concatenate([q_hi, q_lo, q_hi], axis=0)
        out[...] -= dot(left, right, TN)

    def add(slot):
        out[...] += dot(dyall[slot], held[slot], TN)

    def add_piece(slot, first, count):
        some = pl.ds(first * part, count * part)
        out[...] += dot(dyall[slot, some, :], held[slot, some, :], TN)

    last = CHUNKS * steps - 1
    work = [
        (5, p_sum.scatter_dp),
        (8, lambda: send_dyx(0)),
        (9, p_sum.gather_dp),
        (10, lambda: send_dyx(1)),
        (12, p_sum.gather_outer),
        (14, gather_p),
        (16, start_u),
        (18, u_sum.scatter_dp),
        (19, lambda: wait_dyx(1)),
        (19, start_gram),
        (20, lambda: eliminate(0, rank // 2)),
        (21, u_sum.gather_dp),
        (22, lambda: eliminate(rank // 2, rank)),
        (24, u_sum.gather_outer),
        (26, finish_u),
        (28, correct),
    ]
    order = [0] + [slot for d in range(1, steps) for slot in (d, n_z - d)]
    for i, slot in enumerate(order):
        arrived = CHUNKS * min(slot, n_z - slot) + CHUNKS - 1
        work.append((max(19 + i // 2, arrived), functools.partial(add, slot)))
    work.sort(key=lambda entry: entry[0])

    start_w()
    start_p()
    for t in range(CHUNKS, last + 1):
        s, c = t // CHUNKS, t % CHUNKS
        for copy in sends(s - 1, c):
            copy.wait_recv()
        for copy in sends(s, c):
            copy.start()
        for at, do in work:
            if at == t or (t == last and at > last):
                do()
    for c in range(max(RIGHT, CHUNKS - RIGHT)):
        for first, count in ((c, RIGHT), (RIGHT + c, CHUNKS)):
            if first < count:
                for copy in sends(steps - 1, first):
                    copy.wait_recv()
                add_piece(steps, first, 1)
    for s in range(steps):
        for c in range(CHUNKS):
            for copy in sends(s, c):
                copy.wait_send()
    wait_dyz(0)
    wait_dyx(0)
    w_exchange.wait_send()
    v_exchange.wait_send()
    gram_exchange.wait_send()
    p_sum.drain()
    u_sum.drain()


def local(sizes, acts, out_grads, error, q_warm):
    n_g, n_z, n_x = sizes
    tok, cols = acts.shape
    rows = out_grads.shape[1]
    rows_z = rows // n_z
    rank = q_warm.shape[1]

    def reduce_scratch(height, width):
        across = min(n_z, width // 128)
        piece = pltpu.VMEM((n_z, height * across // n_z, width // across), F32)
        whole = pltpu.VMEM((n_g, height, width), F32)
        return [whole, whole, piece, piece, piece, whole]

    anywhere = pl.BlockSpec(memory_space=pl.ANY)
    in_vmem = pl.BlockSpec(memory_space=pltpu.VMEM)
    dma = pltpu.SemaphoreType.DMA
    new_error, q_next = pl.pallas_call(
        functools.partial(kernel, sizes),
        out_shape=(
            pltpu.VMEM((rows_z, cols), F32),
            pltpu.VMEM((rank, cols), F32),
        ),
        in_specs=[anywhere] * 4,
        out_specs=(in_vmem, in_vmem),
        scratch_shapes=[
            pltpu.VMEM((n_z, tok, cols), BF16),
            pltpu.VMEM((tok, rows), BF16),
            pltpu.VMEM((n_z, tok, rows_z), BF16),
            pltpu.VMEM((rank, cols), F32),
            pltpu.VMEM((n_x, rank // n_x, tok + rows_z), F32),
            pltpu.VMEM((n_x, rank // n_x, tok + rows_z), F32),
            pltpu.VMEM((n_x, rank // n_x, tok + rows_z + rows // n_g), F32),
            pltpu.VMEM((n_g, rank, 2 * rank), F32),
            pltpu.VMEM((rank // n_x, rows), F32),
            pltpu.VMEM((rank, rows_z), F32),
            pltpu.VMEM((rank, 2 * rank), F32),
            *reduce_scratch(rank // n_x, rows // n_g),
            *reduce_scratch(rank // n_g, cols),
            dma((5,)),
            dma((2, n_z // 2, CHUNKS)),
            dma((2, n_z // 2, CHUNKS)),
            dma((2,)),
            dma((2, 2)),
            dma((2,)),
            dma((2,)),
            dma((2,)),
            dma((4, 2)),
            dma((4, 2)),
        ],
        compiler_params=pltpu.CompilerParams(
            collective_id=0, has_side_effects=True, vmem_limit_bytes=VMEM * 1024 * 1024
        ),
        cost_estimate=pl.CostEstimate(
            flops=2 * rows_z * cols * tok * n_z, bytes_accessed=2 * tok * (cols + rows) + 8 * rows_z * cols, transcendentals=0
        ),
        name="powersgd_step",
    )(*(pltpu.with_memory_space_constraint(a, pltpu.HBM) for a in (acts, out_grads, error[0], q_warm.T)))
    return new_error[None], q_next.T


def solution(mesh):
    sizes = (mesh.shape["outer"], mesh.shape["dp"], mesh.shape["tensor"])
    in_specs = (
        P(("outer", "dp"), "tensor"),
        P(("outer", "dp"), None),
        P("outer", "dp", "tensor"),
        P("tensor", None),
    )
    out_specs = (P("outer", "dp", "tensor"), P("tensor", None))
    return jax.shard_map(
        functools.partial(local, sizes), mesh=mesh, in_specs=in_specs, out_specs=out_specs, check_vma=False
    )
```

time: 154 us -> 137 us (0.89)
  Pallas kernels: 146 us -> 134 us
  local copies, waits for them, and re-layouts: 6.67 us -> 1.67 us
    pallas_call x1, Pallas kernels: 146 us -> 134 us  [local(): pl.pallas_call(functools.partial(kernel, sizes), out_shape=(pltpu.VMEM((r...]
    unnamed x9 -> x2, local copies, waits for them, and re-layouts: 6.67 us -> 1.67 us
where the time goes in v2:
time: 137 us
  Pallas kernels  134 us (98%)
  local copies, waits for them, and re-layouts  1.67 us (1%)
    pallas_call x1, Pallas kernels, local(): pl.pallas_call(functools.partial(kernel, sizes), out_shape=(pltpu.VMEM((r...  134 us

profile of v2, /device:TPU:1, one launch (start us, length us, event | category | flops | bytes accessed | tf_op | source)
XLA Modules:
  0.0 136.6 jit_solution(16208675534537569906)
XLA Ops:
  0.6 134.3 %powersgd_step.1 = (f32[256,1024]{1,0:T(8,128)S(1)}, f32[64,1024]{1,0:T(8,128)S(1)}) custom-call(bf16[256,1024]{1,0:T(8,128)(2,1)} %acts.1, bf16[256,4096]{1,0:T(8,128)(2,1)} %dy.1, f32[256,1024]{1,0:T(8,128)} %bitcast.6, f32[64,1024]{1,0:T(8,128)} %bitcast.7), custom_call_target="tpu_custom_call" | custom-call | flops 2147483648 | bytes 4718592 | tf_op jit(solution)/shard_map/powersgd_step/pallas_call | solution.py:400
  134.9 1.0 copy.8
  135.9 0.7 copy.9

commit v3 on v2

--- a/solution.py
+++ b/solution.py
@@ -186,7 +186,7 @@
         for copy in sends(0, c):
             copy.start()
 
-    def send_dy(d, carry):
+    def send_dyz(d, carry):
         to = lax.rem(z + d, n_z)
         pltpu.make_async_remote_copy(
             src_ref=dy.at[my_tokens, pl.ds(pl.multiple_of(to * rows_z, rows_z), rows_z)],
@@ -198,7 +198,8 @@
         ).start()
         return carry
 
-    lax.fori_loop(1, n_z, send_dy, 0)
+    def start_dyz():
+        lax.fori_loop(1, n_z, send_dyz, 0)
 
     def wait_dyz(which):
         arrived = dyall.at[pl.ds(1, n_z - 1), pl.ds(0, quarter), :]
@@ -328,31 +329,32 @@
 
     last = CHUNKS * steps - 1
     work = [
-        (5, p_sum.scatter_dp),
-        (8, lambda: send_dyx(0)),
-        (9, p_sum.gather_dp),
-        (10, lambda: send_dyx(1)),
-        (12, p_sum.gather_outer),
-        (14, gather_p),
-        (16, start_u),
-        (18, u_sum.scatter_dp),
-        (19, lambda: wait_dyx(1)),
-        (19, start_gram),
-        (20, lambda: eliminate(0, rank // 2)),
-        (21, u_sum.gather_dp),
-        (22, lambda: eliminate(rank // 2, rank)),
-        (24, u_sum.gather_outer),
-        (26, finish_u),
-        (28, correct),
+        (5, start_p),
+        (7, p_sum.scatter_dp),
+        (10, p_sum.gather_dp),
+        (10, start_dyz),
+        (13, p_sum.gather_outer),
+        (13, gather_p),
+        (13, start_u),
+        (15, u_sum.scatter_dp),
+        (15, start_gram),
+        (16, lambda: send_dyx(0)),
+        (16, lambda: eliminate(0, rank // 2)),
+        (17, lambda: send_dyx(1)),
+        (19, u_sum.gather_dp),
+        (21, lambda: eliminate(rank // 2, rank)),
+        (22, u_sum.gather_outer),
+        (23, lambda: wait_dyx(1)),
+        (25, finish_u),
+        (27, correct),
     ]
     order = [0] + [slot for d in range(1, steps) for slot in (d, n_z - d)]
     for i, slot in enumerate(order):
         arrived = CHUNKS * min(slot, n_z - slot) + CHUNKS - 1
-        work.append((max(19 + i // 2, arrived), functools.partial(add, slot)))
+        work.append((max(23 + i // 2, arrived), functools.partial(add, slot)))
     work.sort(key=lambda entry: entry[0])
 
     start_w()
-    start_p()
     for t in range(CHUNKS, last + 1):
         s, c = t // CHUNKS, t % CHUNKS
         for copy in sends(s - 1, c):

time: 137 us -> 133 us (0.971)
  Pallas kernels: 134 us -> 131 us
    pallas_call x1, Pallas kernels: 134 us -> 131 us  [local(): pl.pallas_call(functools.partial(kernel, sizes), out_shape=(pltpu.VMEM((r...]
where the time goes in v3:
time: 133 us
  Pallas kernels  131 us (98%)
  local copies, waits for them, and re-layouts  1.67 us (1%)
    pallas_call x1, Pallas kernels, local(): pl.pallas_call(functools.partial(kernel, sizes), out_shape=(pltpu.VMEM((r...  131 us

profile of v3, /device:TPU:1, one launch (start us, length us, event | category | flops | bytes accessed | tf_op | source)
XLA Modules:
  0.0 132.9 jit_solution(2886849444100550274)
XLA Ops:
  0.6 130.6 %powersgd_step.1 = (f32[256,1024]{1,0:T(8,128)S(1)}, f32[64,1024]{1,0:T(8,128)S(1)}) custom-call(bf16[256,1024]{1,0:T(8,128)(2,1)} %acts.1, bf16[256,4096]{1,0:T(8,128)(2,1)} %dy.1, f32[256,1024]{1,0:T(8,128)} %bitcast.6, f32[64,1024]{1,0:T(8,128)} %bitcast.7), custom_call_target="tpu_custom_call" | custom-call | flops 2147483648 | bytes 4718592 | tf_op jit(solution)/shard_map/powersgd_step/pallas_call | solution.py:402
  131.2 1.0 copy.8
  132.2 0.7 copy.9

commit v4 on v3

--- a/solution.py
+++ b/solution.py
@@ -8,7 +8,6 @@
 from jax.sharding import PartitionSpec as P
 
 MESH = pl.DeviceIdType.MESH
-VMEM = 62
 CHUNKS = 4
 RIGHT = 2
 F32 = jnp.float32
@@ -38,20 +37,23 @@
 
 
 class Exchange:
-    def __init__(self, axis, n, slots, sems):
-        self.axis, self.n, self.slots, self.sems = axis, n, slots, sems
+    def __init__(self, axis, n, slots, sems, stride=1, shift=0):
+        self.axis, self.n, self.slots, self.sems, self.stride, self.shift = axis, n, slots, sems, stride, shift
+
+    def index(self, place):
+        return lax.rem(place + self.shift, self.n * self.stride) // self.stride
 
     def me(self):
-        return lax.axis_index(self.axis)
+        return self.index(lax.axis_index(self.axis))
 
     def get(self, source):
         return self.slots[lax.rem(self.me() + self.n - source, self.n)]
 
     def start(self, source):
         def send(d, carry):
-            to = lax.rem(self.me() + d, self.n)
+            to = lax.rem(lax.axis_index(self.axis) + d * self.stride, self.n * self.stride)
             pltpu.make_async_remote_copy(
-                src_ref=source(to),
+                src_ref=source(self.index(to)),
                 dst_ref=self.slots.at[d],
                 send_sem=self.sems.at[0],
                 recv_sem=self.sems.at[1],
@@ -124,13 +126,103 @@
             exchange.wait_send()
 
 
+class Pair:
+    def __init__(self, to, slot, sems):
+        self.to, self.slot, self.sems = to, slot, sems
+
+    def start(self, source):
+        pltpu.make_async_remote_copy(
+            src_ref=source,
+            dst_ref=self.slot,
+            send_sem=self.sems.at[0],
+            recv_sem=self.sems.at[1],
+            device_id={"dp": self.to},
+            device_id_type=MESH,
+        ).start()
+
+    def wait_recv(self):
+        pltpu.make_async_copy(self.slot, self.slot, self.sems.at[1]).wait()
+
+    def wait_send(self):
+        pltpu.make_async_copy(self.slot, self.slot, self.sems.at[0]).wait()
+
+
+class PairReduce(Reduce):
+    def __init__(self, n_g, n_z, part, grs, zsrc, zpair, zmid, zrs, zag, zback, gag, sems):
+        self.n_g, self.half, self.part, self.zsrc, self.zmid = n_g, n_z // 2, part, zsrc, zmid
+        self.height, self.width = zsrc.shape[2:]
+        self.across = part.shape[2] // self.width
+        shift = lax.rem(lax.axis_index("outer"), 2)
+        z = lax.axis_index("dp")
+        self.parity = lax.rem(z + shift, 2)
+        partner = lax.rem(z + n_z + 1 - 2 * self.parity, n_z)
+        self.grs = Exchange("outer", n_g, grs, sems.at[0])
+        self.pair = Pair(partner, zpair, sems.at[1])
+        self.zrs = Exchange("dp", self.half, zrs, sems.at[2], 2, shift)
+        self.zag = Exchange("dp", self.half, zag, sems.at[3], 2, shift)
+        self.back = Pair(partner, zback, sems.at[4])
+        self.gag = Exchange("outer", n_g, gag, sems.at[5])
+
+    def place(self, piece):
+        down, right = piece // self.across * self.height, piece % self.across * self.width
+        return slice(down, down + self.height), slice(right, right + self.width)
+
+    def scatter_outer(self):
+        self.grs.start(lambda to: self.part.at[to])
+
+    def swap_dp(self):
+        self.grs.wait_recv()
+        self.grs.slots[0] = self.part[self.grs.me()]
+        total = self.grs.get(0)
+        for source in range(1, self.n_g):
+            total = total + self.grs.get(source)
+        for piece in range(2 * self.half):
+            self.zsrc[piece % 2, piece // 2] = total[self.place(piece)]
+        self.pair.start(self.zsrc.at[1 - self.parity])
+
+    def scatter_dp(self):
+        self.pair.wait_recv()
+        self.zmid[...] = self.zsrc[self.parity] + self.pair.slot[...]
+        self.zrs.start(lambda to: self.zmid.at[to])
+
+    def gather_dp(self):
+        self.zrs.wait_recv()
+        self.zrs.slots[0] = self.zmid[self.zrs.me()]
+        total = self.zrs.get(0)
+        for source in range(1, self.half):
+            total = total + self.zrs.get(source)
+        self.zag.slots[0] = total
+        self.zag.start(lambda to: self.zag.slots.at[0])
+
+    def swap_back(self):
+        self.zag.wait_recv()
+        self.back.start(self.zag.slots)
+
+    def gather_outer(self):
+        self.back.wait_recv()
+        mine = self.zag.me()
+        for piece in range(2 * self.half):
+            slot = lax.rem(mine + self.half - piece // 2, self.half)
+            block = jnp.where(self.parity == piece % 2, self.zag.slots[slot], self.back.slot[slot])
+            self.gag.slots[(0, *self.place(piece))] = block
+        self.gag.start(lambda to: self.gag.slots.at[0])
+
+    def finish(self):
+        self.gag.wait_recv()
+        return [self.gag.get(source) for source in range(self.n_g)]
+
+    def drain(self):
+        for exchange in (self.grs, self.pair, self.zrs, self.zag, self.back, self.gag):
+            exchange.wait_send()
+
+
 def kernel(
     sizes,
     acts, dy, err, q,
     out, q_out,
     held, dyv, dyall, qv, wsrc, wex, vex, gex, pfull, prow, elim,
     part_p, grs_p, zsrc_p, zrs_p, zag_p, gag_p,
-    part_u, grs_u, zsrc_u, zrs_u, zag_u, gag_u,
+    part_u, grs_u, zsrc_u, zpair_u, zmid_u, zrs_u, zag_u, zback_u, gag_u,
     loc, ring_send, ring_recv, dyz_sems, dyx_sems, wex_sems, vex_sems, gram_sems, p_sems, u_sems,
 ):
     n_g, n_z, n_x = sizes
@@ -230,7 +322,7 @@
             pltpu.make_async_copy(arrived, arrived, dyx_sems.at[which, piece]).wait()
 
     p_sum = Reduce(n_g, n_z, part_p, grs_p, zsrc_p, zrs_p, zag_p, gag_p, p_sems)
-    u_sum = Reduce(n_g, n_z, part_u, grs_u, zsrc_u, zrs_u, zag_u, gag_u, u_sems)
+    u_sum = PairReduce(n_g, n_z, part_u, grs_u, zsrc_u, zpair_u, zmid_u, zrs_u, zag_u, zback_u, gag_u, u_sems)
     w_exchange = Exchange("tensor", n_x, wex, wex_sems)
     v_exchange = Exchange("tensor", n_x, vex, vex_sems)
     gram_exchange = Exchange("outer", n_g, gex, gram_sems)
@@ -336,17 +428,19 @@
         (13, p_sum.gather_outer),
         (13, gather_p),
         (13, start_u),
-        (15, u_sum.scatter_dp),
+        (15, u_sum.swap_dp),
         (15, start_gram),
         (16, lambda: send_dyx(0)),
         (16, lambda: eliminate(0, rank // 2)),
         (17, lambda: send_dyx(1)),
-        (19, u_sum.gather_dp),
+        (18, u_sum.scatter_dp),
+        (20, u_sum.gather_dp),
         (21, lambda: eliminate(rank // 2, rank)),
-        (22, u_sum.gather_outer),
         (23, lambda: wait_dyx(1)),
-        (25, finish_u),
-        (27, correct),
+        (23, u_sum.swap_back),
+        (26, u_sum.gather_outer),
+        (28, finish_u),
+        (29, correct),
     ]
     order = [0] + [slot for d in range(1, steps) for slot in (d, n_z - d)]
     for i, slot in enumerate(order):
@@ -383,6 +477,17 @@
     u_sum.drain()
 
 
+def store(new_error, q_next, error_out, q_out, sems):
+    copies = [
+        pltpu.make_async_copy(new_error, error_out, sems.at[0]),
+        pltpu.make_async_copy(q_next, q_out, sems.at[1]),
+    ]
+    for copy in copies:
+        copy.start()
+    for copy in copies:
+        copy.wait()
+
+
 def local(sizes, acts, out_grads, error, q_warm):
     n_g, n_z, n_x = sizes
     tok, cols = acts.shape
@@ -390,11 +495,14 @@
     rows_z = rows // n_z
     rank = q_warm.shape[1]
 
-    def reduce_scratch(height, width):
+    def reduce_scratch(height, width, paired):
         across = min(n_z, width // 128)
-        piece = pltpu.VMEM((n_z, height * across // n_z, width // across), F32)
+        piece = (height * across // n_z, width // across)
         whole = pltpu.VMEM((n_g, height, width), F32)
-        return [whole, whole, piece, piece, piece, whole]
+        pieces, half = pltpu.VMEM((n_z, *piece), F32), pltpu.VMEM((n_z // 2, *piece), F32)
+        if paired:
+            return [whole, whole, pltpu.VMEM((2, n_z // 2, *piece), F32), *[half] * 5, whole]
+        return [whole, whole, *[pieces] * 3, whole]
 
     anywhere = pl.BlockSpec(memory_space=pl.ANY)
     in_vmem = pl.BlockSpec(memory_space=pltpu.VMEM)
@@ -419,8 +527,8 @@
             pltpu.VMEM((rank // n_x, rows), F32),
             pltpu.VMEM((rank, rows_z), F32),
             pltpu.VMEM((rank, 2 * rank), F32),
-            *reduce_scratch(rank // n_x, rows // n_g),
-            *reduce_scratch(rank // n_g, cols),
+            *reduce_scratch(rank // n_x, rows // n_g, False),
+            *reduce_scratch(rank // n_g, cols, True),
             dma((5,)),
             dma((2, n_z // 2, CHUNKS)),
             dma((2, n_z // 2, CHUNKS)),
@@ -430,16 +538,27 @@
             dma((2,)),
             dma((2,)),
             dma((4, 2)),
-            dma((4, 2)),
+            dma((6, 2)),
         ],
         compiler_params=pltpu.CompilerParams(
-            collective_id=0, has_side_effects=True, vmem_limit_bytes=VMEM * 1024 * 1024
+            collective_id=0, has_side_effects=True, vmem_limit_bytes=48 * 1024 * 1024
         ),
         cost_estimate=pl.CostEstimate(
             flops=2 * rows_z * cols * tok * n_z, bytes_accessed=2 * tok * (cols + rows) + 8 * rows_z * cols, transcendentals=0
         ),
         name="powersgd_step",
     )(*(pltpu.with_memory_space_constraint(a, pltpu.HBM) for a in (acts, out_grads, error[0], q_warm.T)))
+    new_error, q_next = pl.pallas_call(
+        store,
+        out_shape=(
+            jax.ShapeDtypeStruct(new_error.shape, F32),
+            jax.ShapeDtypeStruct(q_next.shape, F32),
+        ),
+        in_specs=[in_vmem] * 2,
+        out_specs=(anywhere, anywhere),
+        scratch_shapes=[dma((2,))],
+        name="store_results",
+    )(*(pltpu.with_memory_space_constraint(a, pltpu.VMEM) for a in (new_error, q_next)))
     return new_error[None], q_next.T
 
 

time: 133 us -> 132 us (level)
  local copies, waits for them, and re-layouts: 1.67 us -> 0 us
    unnamed x2 -> x0, local copies, waits for them, and re-layouts: 1.67 us -> none
where the time goes in v4:
time: 132 us
  Pallas kernels  131 us (99%)
    pallas_call x1, Pallas kernels, local(): pl.pallas_call(functools.partial(kernel, sizes), out_shape=(pltpu.VMEM((r...  130 us

profile of v4, /device:TPU:1, one launch (start us, length us, event | category | flops | bytes accessed | tf_op | source)
XLA Modules:
  0.0 131.7 jit_solution(5433803651045522878)
XLA Ops:
  0.6 130.0 %powersgd_step.1 = (f32[256,1024]{1,0:T(8,128)S(1)}, f32[64,1024]{1,0:T(8,128)S(1)}) custom-call(bf16[256,1024]{1,0:T(8,128)(2,1)} %acts.1, bf16[256,4096]{1,0:T(8,128)(2,1)} %dy.1, f32[256,1024]{1,0:T(8,128)} %bitcast.4, f32[64,1024]{1,0:T(8,128)} %bitcast.6), custom_call_target="tpu_custom_call" | custom-call | flops 2147483648 | bytes 4718592 | tf_op jit(solution)/shard_map/powersgd_step/pallas_call | solution.py:510
  130.7 1.1 store_results.1

commit v5 on v4

--- a/solution.py
+++ b/solution.py
@@ -157,10 +157,10 @@
         self.parity = lax.rem(z + shift, 2)
         partner = lax.rem(z + n_z + 1 - 2 * self.parity, n_z)
         self.grs = Exchange("outer", n_g, grs, sems.at[0])
-        self.pair = Pair(partner, zpair, sems.at[1])
+        self.pair = Pair(partner, zpair.at[pl.ds(0, self.half)], sems.at[1])
         self.zrs = Exchange("dp", self.half, zrs, sems.at[2], 2, shift)
         self.zag = Exchange("dp", self.half, zag, sems.at[3], 2, shift)
-        self.back = Pair(partner, zback, sems.at[4])
+        self.back = Pair(partner, zback.at[pl.ds(0, self.half)], sems.at[4])
         self.gag = Exchange("outer", n_g, gag, sems.at[5])
 
     def place(self, piece):
@@ -182,7 +182,8 @@
 
     def scatter_dp(self):
         self.pair.wait_recv()
-        self.zmid[...] = self.zsrc[self.parity] + self.pair.slot[...]
+        for piece in range(self.half):
+            self.zmid[piece] = self.zsrc[self.parity, piece] + self.pair.slot[piece]
         self.zrs.start(lambda to: self.zmid.at[to])
 
     def gather_dp(self):
@@ -196,7 +197,7 @@
 
     def swap_back(self):
         self.zag.wait_recv()
-        self.back.start(self.zag.slots)
+        self.back.start(self.zag.slots.at[pl.ds(0, self.half)])
 
     def gather_outer(self):
         self.back.wait_recv()
@@ -378,8 +379,8 @@
             gram = gram + gram_exchange.get(source)
         row = lax.broadcasted_iota(jnp.int32, (rank, rank), 0)
         col = lax.broadcasted_iota(jnp.int32, (rank, rank), 1)
-        elim[:, :rank] = (row == col).astype(F32)
-        elim[:, rank:] = gram[:, :rank]
+        elim[:rank, :rank] = (row == col).astype(F32)
+        elim[:rank, rank:] = gram[:, :rank]
 
     def eliminate(first, last):
         row = lax.broadcasted_iota(jnp.int32, (rank, 2 * rank), 0)
@@ -387,13 +388,13 @@
         lane1 = lax.broadcasted_iota(jnp.int32, (1, 2 * rank), 1)
 
         def column(j, carry):
-            whole = elim[...]
+            whole = elim[:rank]
             pivot_row = elim[pl.ds(j, 1), :]
             pivot = jnp.sum(jnp.where(lane1 == rank + j, pivot_row, 0.0), axis=1, keepdims=True)
             scale = 1.0 / jnp.sqrt(pivot)
             pivot_row = pivot_row * scale
             factor = jnp.sum(jnp.where(lane == rank + j, whole, 0.0), axis=1, keepdims=True) * scale
-            elim[...] = jnp.where(row > j, whole - factor * pivot_row, jnp.where(row == j, pivot_row, whole))
+            elim[:rank] = jnp.where(row > j, whole - factor * pivot_row, jnp.where(row == j, pivot_row, whole))
             return carry
 
         lax.fori_loop(first, last, column, 0)
@@ -402,7 +403,7 @@
         q_out[...] = jnp.concatenate(u_sum.finish(), axis=0)
 
     def correct():
-        inverse = elim[:, :rank]
+        inverse = elim[:rank, :rank]
         qt = dot(inverse, q_out[...], NN, HIGH) * (1.0 / n_g)
         pt = dot(inverse, prow[...], NN, HIGH)
         q_out[...] = qt
@@ -499,9 +500,9 @@
         across = min(n_z, width // 128)
         piece = (height * across // n_z, width // across)
         whole = pltpu.VMEM((n_g, height, width), F32)
-        pieces, half = pltpu.VMEM((n_z, *piece), F32), pltpu.VMEM((n_z // 2, *piece), F32)
+        pieces, half = pltpu.VMEM((n_z + 1, *piece), F32), pltpu.VMEM((n_z // 2 + 1, *piece), F32)
         if paired:
-            return [whole, whole, pltpu.VMEM((2, n_z // 2, *piece), F32), *[half] * 5, whole]
+            return [whole, whole, pltpu.VMEM((3, n_z // 2, *piece), F32), *[half] * 5, whole]
         return [whole, whole, *[pieces] * 3, whole]
 
     anywhere = pl.BlockSpec(memory_space=pl.ANY)
@@ -526,7 +527,7 @@
             pltpu.VMEM((n_g, rank, 2 * rank), F32),
             pltpu.VMEM((rank // n_x, rows), F32),
             pltpu.VMEM((rank, rows_z), F32),
-            pltpu.VMEM((rank, 2 * rank), F32),
+            pltpu.VMEM((rank + 8, 2 * rank), F32),
             *reduce_scratch(rank // n_x, rows // n_g, False),
             *reduce_scratch(rank // n_g, cols, True),
             dma((5,)),

time: 132 us -> 132 us (level)
  no operation moved by 1% of the time
where the time goes in v5:
time: 132 us
  Pallas kernels  131 us (99%)
    pallas_call x1, Pallas kernels, local(): pl.pallas_call(functools.partial(kernel, sizes), out_shape=(pltpu.VMEM((r...  130 us

profile of v5, /device:TPU:1, one launch (start us, length us, event | category | flops | bytes accessed | tf_op | source)
XLA Modules:
  0.0 131.7 jit_solution(12697248278148193557)
XLA Ops:
  0.6 130.0 %powersgd_step.1 = (f32[256,1024]{1,0:T(8,128)S(1)}, f32[64,1024]{1,0:T(8,128)S(1)}) custom-call(bf16[256,1024]{1,0:T(8,128)(2,1)} %acts.1, bf16[256,4096]{1,0:T(8,128)(2,1)} %dy.1, f32[256,1024]{1,0:T(8,128)} %bitcast.4, f32[64,1024]{1,0:T(8,128)} %bitcast.6), custom_call_target="tpu_custom_call" | custom-call | flops 2147483648 | bytes 4718592 | tf_op jit(solution)/shard_map/powersgd_step/pallas_call | solution.py:511
  130.7 1.1 store_results.1

commit v6 on v5

--- a/solution.py
+++ b/solution.py
@@ -422,10 +422,10 @@
 
     last = CHUNKS * steps - 1
     work = [
-        (5, start_p),
-        (7, p_sum.scatter_dp),
-        (10, p_sum.gather_dp),
-        (10, start_dyz),
+        (4, start_p),
+        (6, p_sum.scatter_dp),
+        (9, p_sum.gather_dp),
+        (9, start_dyz),
         (13, p_sum.gather_outer),
         (13, gather_p),
         (13, start_u),

time: 132 us -> 132 us (level)
  no operation moved by 1% of the time
where the time goes in v6:
time: 132 us; the launch traced here: 131 us
  Pallas kernels  131 us (99%)
    pallas_call x1, Pallas kernels, local(): pl.pallas_call(functools.partial(kernel, sizes), out_shape=(pltpu.VMEM((r...  130 us

profile of v6, /device:TPU:1, one launch (start us, length us, event | category | flops | bytes accessed | tf_op | source)
XLA Modules:
  0.0 131.3 jit_solution(13020705384644400356)
XLA Ops:
  0.6 129.6 %powersgd_step.1 = (f32[256,1024]{1,0:T(8,128)S(1)}, f32[64,1024]{1,0:T(8,128)S(1)}) custom-call(bf16[256,1024]{1,0:T(8,128)(2,1)} %acts.1, bf16[256,4096]{1,0:T(8,128)(2,1)} %dy.1, f32[256,1024]{1,0:T(8,128)} %bitcast.4, f32[64,1024]{1,0:T(8,128)} %bitcast.6), custom_call_target="tpu_custom_call" | custom-call | flops 2147483648 | bytes 4718592 | tf_op jit(solution)/shard_map/powersgd_step/pallas_call | solution.py:511
  130.2 1.1 store_results.1

commit v7 on v5

--- a/solution.py
+++ b/solution.py
@@ -279,7 +279,8 @@
         for copy in sends(0, c):
             copy.start()
 
-    def send_dyz(d, carry):
+    def send_dyz(i, carry):
+        d = (i % 2) * ((i + 1) // 2) + (1 - i % 2) * (n_z - i // 2)
         to = lax.rem(z + d, n_z)
         pltpu.make_async_remote_copy(
             src_ref=dy.at[my_tokens, pl.ds(pl.multiple_of(to * rows_z, rows_z), rows_z)],

time: 132 us -> 132 us (level)
  no operation moved by 1% of the time
where the time goes in v7:
time: 132 us; the launch traced here: 131 us
  Pallas kernels  131 us (99%)
    pallas_call x1, Pallas kernels, local(): pl.pallas_call(functools.partial(kernel, sizes), out_shape=(pltpu.VMEM((r...  130 us

profile of v7, /device:TPU:1, one launch (start us, length us, event | category | flops | bytes accessed | tf_op | source)
XLA Modules:
  0.0 131.3 jit_solution(3722036429155514251)
XLA Ops:
  0.6 129.6 %powersgd_step.1 = (f32[256,1024]{1,0:T(8,128)S(1)}, f32[64,1024]{1,0:T(8,128)S(1)}) custom-call(bf16[256,1024]{1,0:T(8,128)(2,1)} %acts.1, bf16[256,4096]{1,0:T(8,128)(2,1)} %dy.1, f32[256,1024]{1,0:T(8,128)} %bitcast.4, f32[64,1024]{1,0:T(8,128)} %bitcast.6), custom_call_target="tpu_custom_call" | custom-call | flops 2147483648 | bytes 4718592 | tf_op jit(solution)/shard_map/powersgd_step/pallas_call | solution.py:512
  130.2 1.1 store_results.1
